TPU v7x, 512 devices: a whole 4x4x16 slice. The times are simulated.
512 devices in a mesh: video: 128 (over z_lo, x, y), head: 4 (over z_hi, core).
Axes of the slice: x: 4, y: 4, z: 16 (z_hi: 2, z_lo: 8; z = z_hi * 8 + z_lo), core: 2. Of those that a mesh axis runs over, the one named last changes fastest.
Arguments:
- qkv: bfloat16 [128, 768, 3, 1536], P('video', 'head'), may hold values from -50 to 50
- tile_masks: int32 [128, 2, 6, 6], replicated, may hold values 0 or 1
Outputs:
- attended: bfloat16 [128, 768, 1536], P('video', 'head')
All inputs are finite; a program needn't handle non-finite values.
Results may differ from a plain program's by a relative error of at most 0.0036.
Values may be sent and summed in bfloat16 or wider, within the bound.
A program may use at most 64 MiB of HBM per device.

v0:
```python
import jax
import jax.numpy as jnp
from jax import lax
from jax.sharding import PartitionSpec as P

DH = 96
TILE = 128


def passed_along(block, axis, distance):
    devices = range(lax.axis_size(axis))
    route = [((i - distance) % len(devices), i) for i in devices]
    return lax.ppermute(block, axis, route)


def neighbours(kv_block):
    below = passed_along(kv_block, "video", 1)
    above = passed_along(kv_block, "video", -1)
    below_two = passed_along(kv_block, "video", 2)
    above_two = passed_along(kv_block, "video", -2)
    return (below, above, below_two, above_two)


def attend(query, sources, tiles):
    keys = jnp.concatenate([src[:, 0] for src in sources], axis=0)
    values = jnp.concatenate([src[:, 1] for src in sources], axis=0)
    rows = query.shape[0]
    width = query.shape[1]
    count = width // DH
    span = keys.shape[0]
    q_heads = jnp.transpose(query.reshape(rows, count, DH), (1, 0, 2))
    k_heads = jnp.transpose(keys.reshape(span, count, DH), (1, 0, 2))
    v_heads = jnp.transpose(values.reshape(span, count, DH), (1, 0, 2))
    tile_rows = tiles.shape[0]
    tile_cols = tiles.shape[1]
    shown = (tiles > 0)[:, None, :, None]
    scale = DH ** (-0.5)

    def one_head(operands):
        q_head, k_head, v_head = operands
        scores = (
            lax.dot_general(
                q_head, k_head, (((1,), (1,)), ((), ())), preferred_element_type=jnp.float32
            )
            * scale
        )
        scores = scores.reshape(tile_rows, TILE, tile_cols, TILE)
        scores = jnp.where(shown, scores, -jnp.inf).reshape(rows, span)
        top = jnp.max(scores, axis=-1, keepdims=True)
        weights = jnp.exp(scores - top)
        total = jnp.sum(weights, axis=-1, keepdims=True)
        summed = jnp.dot(weights.astype(jnp.bfloat16), v_head, preferred_element_type=jnp.float32)
        return (summed / total).astype(jnp.bfloat16)

    results = lax.map(one_head, (q_heads, k_heads, v_heads))
    return jnp.transpose(results, (1, 0, 2)).reshape(rows, width)


def body(qkv, tile_masks):
    groups = lax.axis_size("head")
    count = lax.axis_size("video")
    place = lax.axis_index("video")
    rows = qkv.shape[1]
    width = qkv.shape[3]
    local = qkv[0].reshape(rows, 3, groups, width // groups)
    arrived = lax.all_to_all(local, "head", split_axis=2, concat_axis=0, tiled=True)
    arrived = arrived.reshape(rows * groups, 3, width // groups)
    query = arrived[:, 0]
    own = arrived[:, 1:3]
    below, above, below_two, above_two = neighbours(own)
    mine = lax.dynamic_index_in_dim(tile_masks, place, 0, keepdims=False)
    left_one = lax.dynamic_index_in_dim(tile_masks, (place + count - 1) % count, 0, keepdims=False)
    left_two = lax.dynamic_index_in_dim(tile_masks, (place + count - 2) % count, 0, keepdims=False)
    ones = jnp.ones_like(mine[0])
    tiles = jnp.concatenate([ones, mine[0], mine[1], left_one[0].T, left_two[1].T], axis=1)
    output = attend(query, [own, above, above_two, below, below_two], tiles)
    returned = lax.all_to_all(output, "head", split_axis=0, concat_axis=1, tiled=True)
    return returned.reshape(1, rows, width)


def solution(mesh):
    placed = (P("video", "head", None, None), P())
    return jax.shard_map(
        body, mesh=mesh, in_specs=placed, out_specs=P("video", "head", None), check_vma=False
    )
```

profile of v0, /device:TPU:152, one launch (start us, length us, event | category | flops | bytes accessed | tf_op | source)
XLA Modules:
  0.0 376.6 jit_solution(3412624409843682443)
XLA Ops:
  0.0 3.2 reshape_squeeze.6
  3.5 86.8 %all_to_all.31 = bf16[192,3,4,384]{3,0,1,2:T(8,128)(2,1)S(1)} all-to-all(bf16[192,3,4,384]{3,0,1,2:T(8,128)(2,1)S(1)} %copy.63), channel_id=1, replica_groups=mesh['video'=128,'head'=4] {'head'}, dimensions={2} | all-to-all | bytes 3538944 | tf_op jit(solution)/shard_map/all_to_all | solution.py:66
  91.6 2.6 collective-permute-start
  94.3 84.9 %collective-permute-start.1 = (bf16[768,2,384]{2,0,1:T(8,128)(2,1)}, bf16[768,2,384]{2,0,1:T(8,128)(2,1)}, u32[]{:S(2)}, u32[]{:S(2)}) collective-permute-start(bf16[768,2,384]{2,0,1:T(8,128)(2,1)} %slice.72), channel_id=1, source_target_pairs={{8,0},{12,4},{16,8},{20,12},{24,16},{28,20},{32,24},{36,28},{40,32... | collective-permute-start | bytes 3538952 | tf_op jit(solution)/shard_map/ppermute | solution.py:13
  190.1 2.4 fusion.30
  193.7 2.5 fusion.29
  196.2 2.1 copy.73
  198.3 89.6 %collective-permute-done.2 = bf16[768,2,384]{2,0,1:T(8,128)(2,1)} collective-permute-done((bf16[768,2,384]{2,0,1:T(8,128)(2,1)}, bf16[768,2,384]{2,0,1:T(8,128)(2,1)}, u32[]{:S(2)}, u32[]{:S(2)}) %collective-permute-start.2) | collective-permute-done | bytes 1179680 | tf_op jit(solution)/shard_map/ppermute | solution.py:13
  287.9 2.4 fusion.28
  290.3 2.1 copy.74
  292.4 2.4 fusion.27
  297.0 2.1 copy.67
  299.1 2.1 copy.68
  303.3 2.1 copy.70
  310.4 42.5 %while.10 = (s32[]{:T(128)}, bf16[4,768,96]{1,2,0:T(8,128)(2,1)S(1)}, pred[6,1,30,1]{2,0,3,1:T(8,128)(4,1)S(1)}, bf16[4,768,96]{1,2,0:T(8,128)(2,1)}, bf16[4,384...) while((s32[]{:T(128)}, bf16[4,768,96]{1,2,0:T(8,128)(2,1)S(1)}, ...), condition=%wide.region_3.4_spmd, body=%wide.region_0.3_spmd.sunk | while | flops 1153251840 | bytes 43076864 | solution.py:55
  311.2 5.7 %fusion.38 = (f32[768]{0:T(1024)S(1)}, f32[768,3840]{1,0:T(8,128)S(1)}) fusion(bf16[4,3840,96]{1,2,0:T(8,128)(2,1)} %get-tuple-element.152, s32[]{:T(128)} %get-tuple-element.141, bf16[4,768,96]{1,2,0:T(8,128)(2,1)} %get-tuple-element.151, pred[96,8,30,128]{3,2,1,0:T(8,128)(4,1)S(1)} %bitcast.75), kind=kOutput, calls=%fused_computation.33.clone.1 | convolution fusion | flops 575077632 | bytes 15634432 | tf_op jit(solution)/shard_map/while/body/eval_jaxpr/dot_general | solution.py:42
  318.8 2.2 fusion.40
  321.9 5.7 %fusion.38 = (f32[768]{0:T(1024)S(1)}, f32[768,3840]{1,0:T(8,128)S(1)}) fusion(bf16[4,3840,96]{1,2,0:T(8,128)(2,1)} %get-tuple-element.152, s32[]{:T(128)} %get-tuple-element.141, bf16[4,768,96]{1,2,0:T(8,128)(2,1)} %get-tuple-element.151, pred[96,8,30,128]{3,2,1,0:T(8,128)(4,1)S(1)} %bitcast.75), kind=kOutput, calls=%fused_computation.33.clone.1 | convolution fusion | flops 575077632 | bytes 15634432 | tf_op jit(solution)/shard_map/while/body/eval_jaxpr/dot_general | solution.py:42
  329.4 2.2 fusion.40
  332.5 5.7 %fusion.38 = (f32[768]{0:T(1024)S(1)}, f32[768,3840]{1,0:T(8,128)S(1)}) fusion(bf16[4,3840,96]{1,2,0:T(8,128)(2,1)} %get-tuple-element.152, s32[]{:T(128)} %get-tuple-element.141, bf16[4,768,96]{1,2,0:T(8,128)(2,1)} %get-tuple-element.151, pred[96,8,30,128]{3,2,1,0:T(8,128)(4,1)S(1)} %bitcast.75), kind=kOutput, calls=%fused_computation.33.clone.1 | convolution fusion | flops 575077632 | bytes 15634432 | tf_op jit(solution)/shard_map/while/body/eval_jaxpr/dot_general | solution.py:42
  340.0 2.2 fusion.40
  343.1 5.7 %fusion.38 = (f32[768]{0:T(1024)S(1)}, f32[768,3840]{1,0:T(8,128)S(1)}) fusion(bf16[4,3840,96]{1,2,0:T(8,128)(2,1)} %get-tuple-element.152, s32[]{:T(128)} %get-tuple-element.141, bf16[4,768,96]{1,2,0:T(8,128)(2,1)} %get-tuple-element.151, pred[96,8,30,128]{3,2,1,0:T(8,128)(4,1)S(1)} %bitcast.75), kind=kOutput, calls=%fused_computation.33.clone.1 | convolution fusion | flops 575077632 | bytes 15634432 | tf_op jit(solution)/shard_map/while/body/eval_jaxpr/dot_general | solution.py:42
  350.6 2.2 fusion.40
  354.5 20.6 %all_to_all.32 = bf16[4,192,384]{2,1,0:T(8,128)(2,1)S(1)} all-to-all(bf16[4,192,384]{2,1,0:T(8,128)(2,1)S(1)} %copy.86), channel_id=1, replica_groups=mesh['video'=128,'head'=4] {'head'}, dimensions={0} | all-to-all | bytes 1179648 | tf_op jit(solution)/shard_map/all_to_all | solution.py:77
  (67 shorter events, 36.3 us)
Async XLA Ops:
  90.3 88.9 %copy-start.6 = (s32[128,2,6,6]{0,1,3,2:T(2,128)S(1)}, s32[128,2,6,6]{0,1,3,2:T(2,128)}, u32[]{:S(2)}) copy-start(s32[128,2,6,6]{0,1,3,2:T(2,128)} %param.5) | copy-start | bytes 110596
  91.6 98.4 %collective-permute-start = (bf16[768,2,384]{2,0,1:T(8,128)(2,1)}, bf16[768,2,384]{2,0,1:T(8,128)(2,1)}, u32[]{:S(2)}, u32[]{:S(2)}) collective-permute-start(bf16[768,2,384]{2,0,1:T(8,128)(2,1)} %slice.72), channel_id=1, source_target_pairs={{4,0},{8,4},{12,8},{16,12},{20,16},{24,20},{28,24},{32,28},{36,32}... | collective-permute-start | bytes 3538952 | tf_op jit(solution)/shard_map/ppermute | solution.py:13
  94.3 99.5 %collective-permute-start.1 = (bf16[768,2,384]{2,0,1:T(8,128)(2,1)}, bf16[768,2,384]{2,0,1:T(8,128)(2,1)}, u32[]{:S(2)}, u32[]{:S(2)}) collective-permute-start(bf16[768,2,384]{2,0,1:T(8,128)(2,1)} %slice.72), channel_id=1, source_target_pairs={{8,0},{12,4},{16,8},{20,12},{24,16},{28,20},{32,24},{36,28},{40,32... | collective-permute-start | bytes 3538952 | tf_op jit(solution)/shard_map/ppermute | solution.py:13
  181.3 106.6 %collective-permute-start.2 = (bf16[768,2,384]{2,0,1:T(8,128)(2,1)}, bf16[768,2,384]{2,0,1:T(8,128)(2,1)}, u32[]{:S(2)}, u32[]{:S(2)}) collective-permute-start(bf16[768,2,384]{2,0,1:T(8,128)(2,1)} %slice.72), channel_id=1, source_target_pairs={{508,0},{0,4},{4,8},{8,12},{12,16},{16,20},{20,24},{24,28},{28,32}... | collective-permute-start | bytes 3538952 | tf_op jit(solution)/shard_map/ppermute | solution.py:13
  183.3 109.2 %collective-permute-start.3 = (bf16[768,2,384]{2,0,1:T(8,128)(2,1)}, bf16[768,2,384]{2,0,1:T(8,128)(2,1)}, u32[]{:S(2)}, u32[]{:S(2)}) collective-permute-start(bf16[768,2,384]{2,0,1:T(8,128)(2,1)} %slice.72), channel_id=1, source_target_pairs={{504,0},{508,4},{0,8},{4,12},{8,16},{12,20},{16,24},{20,28},{24,32... | collective-permute-start | bytes 3538952 | tf_op jit(solution)/shard_map/ppermute | solution.py:13
  305.5 2.9 copy-start.1
  305.5 3.0 copy-start
  305.5 3.0 copy-start.7
  305.5 3.0 copy-start.2
  305.5 3.0 copy-start.3
  306.8 1.9 copy-start.4
  308.4 2.0 copy-start.5
  308.7 1.6 copy-start.8
where the time goes:
time: 378 us; the launch traced here: 377 us
  blocking collectives  107 us (28%)
  starting transfers between devices  91.5 us (24%)
  waiting for transfers between devices  89.6 us (24%)
  local copies, waits for them, and re-layouts  48.7 us (13%)
  matrix products  31.8 us (8%)
  other arithmetic  7.05 us (2%)
    ppermute x4, starting transfers between devices, passed_along(): return lax.ppermute(block, axis, route)  91.5 us
    ppermute x4, waiting for transfers between devices, passed_along(): return lax.ppermute(block, axis, route)  89.6 us
    all_to_all x1, blocking collectives, body(): lax.all_to_all(local, 'head', split_axis=2, concat_axis=0, tiled=True)  86.8 us
    dot_general x4, matrix products, one_head(): lax.dot_general(q_head, k_head, (((1,), (1,)), ((), ())), preferred_eleme...  23 us
    all_to_all x1, blocking collectives, body(): lax.all_to_all(output, 'head', split_axis=0, concat_axis=1, tiled=True)  20.6 us
    slice x10, local copies, waits for them, and re-layouts, attend(): values = jnp.concatenate([src[:, 1] for src in sources], axis=0)  18.6 us
    dot_general x4, matrix products, one_head(): jnp.dot(weights.astype(jnp.bfloat16), v_head, preferred_element_type=jnp....  8.8 us
    slice x5, local copies, waits for them, and re-layouts, attend(): keys = jnp.concatenate([src[:, 0] for src in sources], axis=0)  8.76 us
  transfers between devices with their start and end apart: 4, of which 1 were waited for; matrix products, arithmetic and copies ran while one was open for 5% of the time, Pallas kernels for 0%

commit v1 on v0

v1 whole, which is shorter than its diff:
```python
import functools

import jax
import jax.numpy as jnp
from jax import lax
from jax.experimental import pallas as pl
from jax.experimental.pallas import tpu as pltpu
from jax.sharding import PartitionSpec as P

MESH = pl.DeviceIdType.MESH
DH = 96
TILE = 128
ROWS = 192
TOK = 768
TILES = TOK // TILE
WIDTH = 384
PAIR = 256
SUB = 64
KEYS = 256
SCALE = DH ** (-0.5) * 1.4426950408889634
OWN, MATE, FAR, CROSS = 3, 2, 0, 1


def kernel(x_ref, masks_ref, out_ref, kv, q, obuf, scores, top, total, acc, masks, seen, bias,
           local_sem, ex_send, ex_recv, nb_send, nb_recv, fw_send, fw_recv, ret_send, ret_recv):
    video = lax.axis_index("video")
    group = lax.axis_index("head")
    videos = lax.axis_size("video")
    half, core = group // 2, group % 2
    up = lax.rem(video + 1, videos)
    down = lax.rem(video + videos - 1, videos)

    def group_of(who):
        if isinstance(who, int):
            far, crossed = int(who in (FAR, CROSS)), int(who in (CROSS, MATE))
        else:
            far, crossed = 1 - who // 2, lax.rem(lax.rem(who, 2) + who // 2, 2)
            crossed = jnp.where(who < 2, lax.rem(who, 2), 1 - lax.rem(who, 2))
        return lax.rem(half + far, 2) * 2 + lax.rem(core + crossed, 2)

    def device(who):
        return {"video": video, "head": group_of(who)}

    def along(direction):
        return {"video": (down, up)[direction], "head": group}

    def rows(who):
        return pl.ds(pl.multiple_of(group_of(who) * ROWS, SUB), ROWS)

    def columns(who):
        return pl.ds(pl.multiple_of(group_of(who) * WIDTH, 128), WIDTH)

    here = rows(OWN)
    copies = []

    own_kv = pltpu.make_async_copy(x_ref.at[pl.ds(1, 2), :, columns(OWN)], kv.at[0, :, here], local_sem.at[0])
    own_q = pltpu.make_async_copy(x_ref.at[0, :, columns(OWN)], q.at[here], local_sem.at[1])
    get_masks = pltpu.make_async_copy(masks_ref, masks, local_sem.at[2])
    barrier = pltpu.get_barrier_semaphore()
    for who in (FAR, CROSS, MATE):
        pl.semaphore_signal(barrier, inc=1, device_id=device(who), device_id_type=MESH)
    for direction in (0, 1):
        pl.semaphore_signal(barrier, inc=1, device_id=along(direction), device_id_type=MESH)
    get_masks.start()
    own_kv.start()
    own_q.start()
    pl.semaphore_wait(barrier, 5)

    def remote(src, dst, send, recv, to):
        return pltpu.make_async_remote_copy(
            src_ref=src, dst_ref=dst, send_sem=send, recv_sem=recv, device_id=to, device_id_type=MESH)

    def give_kv(who):
        return remote(x_ref.at[pl.ds(1, 2), :, columns(who)], kv.at[0, :, here], ex_send.at[0, who], ex_recv.at[0, who], device(who))

    def give_q(who):
        return remote(x_ref.at[0, :, columns(who)], q.at[here], ex_send.at[1, who], ex_recv.at[1, who], device(who))

    def take_kv(who):
        return remote(x_ref.at[pl.ds(1, 2), :, columns(who)], kv.at[0, :, rows(who)], ex_send.at[0, who], ex_recv.at[0, who], device(who))

    def take_q(who):
        return remote(x_ref.at[0, :, columns(OWN)], q.at[rows(who)], ex_send.at[1, who], ex_recv.at[1, who], device(who))

    first, second = (1, 3), (2, 4)

    def to_neighbour(who, direction):
        src = x_ref.at[pl.ds(1, 2), :, columns(OWN)] if who == OWN else kv.at[0, :, rows(who)]
        return remote(src, kv.at[first[direction], :, rows(who)], nb_send.at[direction, who], nb_recv.at[direction, who], along(direction))

    def pass_on(who, direction):
        return remote(kv.at[first[direction], :, rows(who)], kv.at[second[direction], :, rows(who)],
                      fw_send.at[direction, who], fw_recv.at[direction, who], along(direction))

    def start(copy):
        copy.start()
        copies.append(copy)

    start(give_kv(MATE))
    for direction in (0, 1):
        start(to_neighbour(OWN, direction))
    start(give_kv(FAR))
    start(give_kv(CROSS))
    start(give_q(FAR))
    start(give_q(CROSS))
    start(give_q(MATE))

    get_masks.wait()
    lane = lax.broadcasted_iota(jnp.int32, (TILES, TILES, 2, 128), 3)
    for back in (0, 1, 2):
        who = lax.rem(video + videos - back, videos)
        value = jnp.sum(jnp.where(lane == who, masks[...].astype(jnp.float32), 0.0), axis=3, keepdims=True)
        seen[back] = jnp.broadcast_to(jnp.where(value > 0.5, 0.0, -jnp.inf), (TILES, TILES, 2, 128))
    bias[0] = jnp.zeros((TILES, TILES, 128), jnp.float32)
    for i in range(TILES):
        bias[1, i] = seen[0, i, :, 0, :]
        bias[2, i] = seen[0, i, :, 1, :]
        bias[3, i] = seen[1, :, i, 0, :]
        bias[4, i] = seen[2, :, i, 1, :]

    def hand_out(who):
        take_kv(who).wait_recv()
        for direction in (0, 1):
            start(to_neighbour(who, direction))

    def hand_on(who):
        for direction in (0, 1):
            to_neighbour(who, direction).wait_recv()
            start(pass_on(who, direction))

    hand_out(MATE)
    hand_on(OWN)
    hand_on(MATE)
    hand_out(FAR)
    hand_on(FAR)
    hand_out(CROSS)
    hand_on(CROSS)
    own_kv.wait()
    own_q.wait()
    for who in (OWN, MATE, FAR, CROSS):
        for direction in (0, 1):
            pass_on(who, direction).wait_recv()

    stacked = 2 * ROWS

    def attend(block, slot):
        for pair in (0, 1):
            lanes = pl.ds(128 * pair, PAIR)
            base = (0, 64)[pair]
            at = lax.broadcasted_iota(jnp.int32, (ROWS, PAIR), 1)
            qp = q[pl.ds(pl.multiple_of(block * ROWS, SUB), ROWS), lanes]
            heads = [jnp.where((at >= base + DH * n) & (at < base + DH * (n + 1)), qp, jnp.zeros_like(qp)) for n in (0, 1)]
            qs = jnp.concatenate(heads, axis=0)
            top[...] = jnp.full((stacked, 128), -jnp.inf, jnp.float32)

            def score(s, _):
                for kb in range(TOK // KEYS):
                    k = kv[s, 0, pl.ds(kb * KEYS, KEYS), lanes]
                    sc = lax.dot_general(qs, k, (((1,), (1,)), ((), ())), preferred_element_type=jnp.float32)
                    cols = []
                    for kt in range(KEYS // 128):
                        parts = []
                        for sub in range(ROWS // SUB):
                            tile = (block * (ROWS // SUB) + sub) // (TILE // SUB)
                            row = bias[s, tile, pl.ds(kb * (KEYS // 128) + kt, 1), :]
                            parts.append(jnp.broadcast_to(row, (SUB, 128)))
                        cols.append(jnp.concatenate(parts * 2, axis=0))
                    sc = sc + jnp.concatenate(cols, axis=1)
                    scores[s * (TOK // KEYS) + kb] = sc
                    top[...] = jnp.maximum(top[...], jnp.maximum(sc[:, :128], sc[:, 128:]))
                return 0

            lax.fori_loop(0, 5, score, 0)
            top[...] = jnp.broadcast_to(jnp.max(top[...], axis=1, keepdims=True), (stacked, 128))
            total[...] = jnp.zeros((stacked, 128), jnp.float32)
            acc[...] = jnp.zeros((stacked, PAIR), jnp.float32)

            def weigh(s, _):
                ws = []
                highest = top[...]
                both = jnp.concatenate([highest, highest], axis=1)
                for kb in range(TOK // KEYS):
                    w = jnp.exp2((scores[s * (TOK // KEYS) + kb] - both) * SCALE)
                    total[...] += w[:, :128] + w[:, 128:]
                    ws.append(w.astype(jnp.bfloat16))
                acc[...] += jnp.dot(jnp.concatenate(ws, axis=1), kv[s, 1, :, lanes], preferred_element_type=jnp.float32)
                return 0

            lax.fori_loop(0, 5, weigh, 0)
            o = acc[...] / jnp.sum(total[...], axis=1, keepdims=True)
            o = jnp.where(at < base + DH, o[:ROWS], o[ROWS:])
            if pair == 1:
                o = jnp.concatenate([
                    jnp.where(at[:, :128] < 64, obuf[slot, :, pl.ds(128, 128)].astype(jnp.float32), o[:, :128]),
                    o[:, 128:]], axis=1)
            obuf[slot, :, lanes] = o.astype(jnp.bfloat16)

    def give_back(who):
        return remote(obuf.at[who], out_ref.at[:, columns(OWN)], ret_send.at[who], ret_recv.at[who], device(who))

    def take_back(who):
        return remote(obuf.at[who], out_ref.at[:, columns(who)], ret_send.at[who], ret_recv.at[who], device(who))

    keep = pltpu.make_async_copy(obuf.at[OWN], out_ref.at[:, columns(OWN)], local_sem.at[3])

    def piece(who, _):
        for other in (FAR, CROSS, MATE):
            pl.when(who == other)(lambda other=other: take_q(other).wait_recv())
        attend(group_of(who), who)
        for other in (FAR, CROSS, MATE):
            pl.when(who == other)(lambda other=other: give_back(other).start())
        pl.when(who == OWN)(keep.start)
        return 0

    lax.fori_loop(0, 4, piece, 0)

    for who in (FAR, CROSS, MATE):
        take_back(who).wait_recv()
        give_back(who).wait_send()
    keep.wait()
    for copy in copies:
        copy.wait_send()


def body(qkv, tile_masks):
    x = jnp.transpose(qkv[0], (1, 0, 2))
    masks = jnp.transpose(tile_masks, (2, 3, 1, 0))
    dma = pltpu.SemaphoreType.DMA
    stacked = 2 * ROWS
    out = pl.pallas_call(
        kernel,
        out_shape=jax.ShapeDtypeStruct((ROWS, x.shape[2]), jnp.bfloat16),
        in_specs=[pl.BlockSpec(memory_space=pl.ANY)] * 2,
        out_specs=pl.BlockSpec(memory_space=pl.ANY),
        scratch_shapes=[
            pltpu.VMEM((5, 2, TOK, WIDTH), jnp.bfloat16),
            pltpu.VMEM((TOK, WIDTH), jnp.bfloat16),
            pltpu.VMEM((4, ROWS, WIDTH), jnp.bfloat16),
            pltpu.VMEM((5 * TOK // KEYS, stacked, KEYS), jnp.float32),
            pltpu.VMEM((stacked, 128), jnp.float32),
            pltpu.VMEM((stacked, 128), jnp.float32),
            pltpu.VMEM((stacked, PAIR), jnp.float32),
            pltpu.VMEM(masks.shape, jnp.int32),
            pltpu.VMEM((3, TILES, TILES, 2, 128), jnp.float32),
            pltpu.VMEM((5, TILES, TILES, 128), jnp.float32),
            dma((4,)),
            dma((2, 3)), dma((2, 3)),
            dma((2, 4)), dma((2, 4)),
            dma((2, 4)), dma((2, 4)),
            dma((3,)), dma((3,)),
        ],
        compiler_params=pltpu.CompilerParams(collective_id=1, has_side_effects=True, vmem_limit_bytes=48 * 2**20),
        name="orbit_attention",
    )(x, masks)
    return out[None]


def solution(mesh):
    placed = (P("video", "head", None, None), P())
    return jax.shard_map(
        body, mesh=mesh, in_specs=placed, out_specs=P("video", "head", None), check_vma=False
    )
```

time: 378 us -> 192 us (0.51)
  the two profiles are of different devices: /device:TPU:152 before, /device:TPU:1 now
where the time goes in v1:
time: 192 us
  Pallas kernels  188 us (98%)
  local copies, waits for them, and re-layouts  3.06 us (2%)
    pallas_call x1, Pallas kernels, body(): pl.pallas_call(kernel, out_shape=jax.ShapeDtypeStruct((ROWS, x.shape[2]),...  188 us

profile of v1, /device:TPU:1, one launch (start us, length us, event | category | flops | bytes accessed | tf_op | source)
XLA Modules:
  0.0 191.5 jit_solution(17345012424784913424)
XLA Ops:
  0.0 0.0 copy-start
  0.0 1.5 copy-done
  1.5 0.0 copy-start.1
  1.5 0.8 copy-done.1
  2.2 188.4 %orbit_attention.1 = bf16[192,1536]{1,0:T(8,128)(2,1)S(1)} custom-call(bf16[3,192,1536]{2,1,0:T(8,128)(2,1)S(1)} %bitcast.6, s32[6,6,2,128]{3,2,1,0:T(2,128)S(1)} %bitcast.7), custom_call_target="tpu_custom_call" | custom-call | tf_op jit(solution)/shard_map/orbit_attention/pallas_call | solution.py:230
  190.7 0.8 copy.4
Async XLA Ops:
  0.0 1.5 copy-start
  1.5 0.8 copy-start.1

commit v2 on v0

v2 whole, which is shorter than its diff:
```python
import jax
import jax.numpy as jnp
from jax import lax
from jax.experimental import pallas as pl
from jax.experimental.pallas import tpu as pltpu
from jax.sharding import PartitionSpec as P

MESH = pl.DeviceIdType.MESH
DH = 96
TILE = 128
ROWS = 192
HALF = 384
TILES = 6
HTILES = HALF // TILE
WIDTH = 384
PAIR = 256
KEYS = 256
SPAN = 2048
STEPS = 4
SCALE = DH ** (-0.5) * 1.4426950408889634
OWN, MATE = 0, 1
FAR, CROSS = 0, 1
PLANE = 16
SIDE = 4
EDGE = (0, PLANE - 1)


def kernel(x_ref, masks_ref, out_ref, kv, q, part, partial_in, near, fin, stat, stat_out, stat_in, scores, top, total, acc,
           masks, seen, bias, held, local_sem, mate_send, mate_recv, far_send, far_recv, nb_send, nb_recv, fw_send, fw_recv,
           hop_send, hop_recv, back_send, back_recv, fin_send, fin_recv):
    video = lax.axis_index("video")
    group = lax.axis_index("head")
    videos = lax.axis_size("video")
    half, core = group // 2, lax.rem(group, 2)
    other_half, other_core = 1 - half, 1 - core
    up = lax.rem(video + 1, videos)
    down = lax.rem(video + videos - 1, videos)
    planes = videos // PLANE
    plane, column = video // PLANE, lax.rem(video, PLANE)
    across, row = column // SIDE, lax.rem(column, SIDE)

    mate = {"video": video, "head": half * 2 + other_core}
    far = ({"video": video, "head": other_half * 2 + core}, {"video": video, "head": other_half * 2 + other_core})

    def along(direction):
        return {"video": (down, up)[direction], "head": group}

    def at_column(level, col):
        return {"video": lax.rem(level + planes, planes) * PLANE + col, "head": group}

    def columns(of_core, n):
        return pl.ds(pl.multiple_of((of_core * 2 + n) * WIDTH, 128), WIDTH)

    def rows(of_core, slot=0):
        return pl.ds(pl.multiple_of(slot * HALF + of_core * ROWS, 64), ROWS)

    both = pl.ds(1, 2)
    core_of = (core, other_core)

    def remote(src, dst, send, recv, to):
        return pltpu.make_async_remote_copy(
            src_ref=src, dst_ref=dst, send_sem=send, recv_sem=recv, device_id=to, device_id_type=MESH)

    copies = []

    def start(copy):
        copy.start()
        copies.append(copy)

    get_masks = pltpu.make_async_copy(masks_ref, masks, local_sem.at[0])
    own_kv = [pltpu.make_async_copy(x_ref.at[both, :, columns(core, n)], kv.at[n, :, rows(core)], local_sem.at[1 + n]) for n in (0, 1)]
    own_q = [pltpu.make_async_copy(x_ref.at[0, :, columns(core, n)], q.at[2 + n, rows(core)], local_sem.at[3 + n]) for n in (0, 1)]
    get_masks.start()
    for copy in own_kv + own_q:
        copy.start()

    barrier = pltpu.get_barrier_semaphore()

    def greet(to):
        pl.semaphore_signal(barrier, inc=1, device_id=to, device_id_type=MESH)

    for to in (*far, mate, along(0), along(1)):
        greet(to)

    relays_up = (row == SIDE - 1) & (across != SIDE - 1)
    relays_down = (row == 0) & (across != 0)
    relaying = relays_up | relays_down
    expected = 5 + relaying.astype(jnp.int32)
    for direction, role in ((0, relays_down), (1, relays_up)):
        pl.when(role)(lambda direction=direction: greet(at_column(plane, EDGE[direction])))

        @pl.when(column == EDGE[1 - direction])
        def _():
            for place in range(SIDE):
                col = place * SIDE + EDGE[direction] % SIDE
                if col != EDGE[direction]:
                    greet(at_column(plane + (1, -1)[direction], col))

        expected += jnp.where(column == EDGE[direction], SIDE - 1, 0)

    pl.semaphore_wait(barrier, expected)

    def mate_kv(n):
        return remote(x_ref.at[both, :, columns(other_core, n)], kv.at[n, :, rows(core)], mate_send.at[0, n], mate_recv.at[0, n], mate)

    def mate_q(n):
        return remote(x_ref.at[0, :, columns(other_core, n)], q.at[2 + n, rows(core)], mate_send.at[1, n], mate_recv.at[1, n], mate)

    def far_q(n, which):
        return remote(x_ref.at[0, :, columns(core_of[which], n)], q.at[n, rows(core)], far_send.at[n, which], far_recv.at[n, which], far[which])

    slots = ((1, 3), (2, 4))

    def source_of(kind, n, block, direction):
        if kind:
            return kv.at[n, :, rows(core_of[block], slots[0][direction])]
        if block == OWN:
            return x_ref.at[both, :, columns(core, n)]
        return kv.at[n, :, rows(other_core)]

    def sems(kind, n, block, direction):
        send, recv = ((nb_send, nb_recv), (fw_send, fw_recv))[kind]
        return send.at[direction, n, block], recv.at[direction, n, block]

    def target_of(kind, n, block, direction):
        return kv.at[n, :, rows(core_of[block], slots[kind][direction])]

    def passing(kind, n, block, direction):
        return remote(source_of(kind, n, block, direction), target_of(kind, n, block, direction),
                      *sems(kind, n, block, direction), along(direction))

    def step(kind, n, block, direction):
        pl.when(column != EDGE[direction])(passing(kind, n, block, direction).start)

        @pl.when(column == EDGE[direction])
        def _():
            send, recv = sems(kind, n, block, direction)
            for which in (0, 1):
                place = block * 2 + which
                col = place * SIDE + EDGE[direction] % SIDE
                src = source_of(kind, n, block, direction).at[which]
                if col == EDGE[direction]:
                    remote(src, target_of(kind, n, block, direction).at[which], send, recv, along(direction)).start()
                else:
                    remote(src, held.at[kind, n], send, hop_recv.at[kind, n], at_column(plane, col)).start()

    def hop(kind, n):
        upward = relays_up.astype(jnp.int32)
        block, which = across // 2, lax.rem(across, 2)
        slot = jnp.where(relays_up, slots[kind][1], slots[kind][0])
        to_rows = rows(lax.rem(core + block, 2), slot)
        recv = (nb_recv, fw_recv)[kind].at[upward, n, block]
        to = at_column(plane + 2 * upward - 1, jnp.where(relays_up, EDGE[0], EDGE[1]))
        return remote(held.at[kind, n], kv.at[n, which, to_rows], hop_send.at[kind, n], recv, to)

    def relay(kind, n):
        @pl.when(relaying)
        def _():
            remote(held.at[kind, n], held.at[kind, n], hop_send.at[kind, n], hop_recv.at[kind, n], along(0)).wait_recv()
            hop(kind, n).start()

    def hand_on(n, direction):
        for block in (OWN, MATE):
            passing(0, n, block, direction).wait_recv()
            step(1, n, block, direction)

    def hand_on_early(n):
        pl.when(column != EDGE[1])(lambda: hand_on(n, 0))
        pl.when(column != EDGE[0])(lambda: hand_on(n, 1))

    def hand_on_late(n):
        pl.when(column == EDGE[1])(lambda: hand_on(n, 0))
        pl.when(column == EDGE[0])(lambda: hand_on(n, 1))

    def give(n, block):
        for direction in (0, 1):
            step(0, n, block, direction)

    def take_mate_kv(n):
        remote(x_ref.at[both, :, columns(core, n)], kv.at[n, :, rows(other_core)], mate_send.at[0, n], mate_recv.at[0, n], mate).wait_recv()

    start(mate_kv(0))
    give(0, OWN)
    start(mate_kv(1))
    start(mate_q(0))
    start(mate_q(1))
    take_mate_kv(0)
    give(0, MATE)
    relay(0, 0)
    start(far_q(0, FAR))

    get_masks.wait()
    lane = lax.broadcasted_iota(jnp.int32, (TILES, TILES, 2, 128), 3)
    for back in (0, 1, 2):
        who = lax.rem(video + videos - back, videos)
        value = jnp.sum(jnp.where(lane == who, masks[...].astype(jnp.float32), 0.0), axis=3, keepdims=True)
        seen[back] = jnp.broadcast_to(jnp.where(value > 0.5, 0.0, -jnp.inf), (TILES, TILES, 2, 128))
    for t in range(HTILES):
        j = half * HTILES + t
        bias[t] = jnp.zeros((TILES, 128), jnp.float32)
        bias[HTILES + t] = seen[0, :, j, 0, :]
        bias[2 * HTILES + t] = seen[0, :, j, 1, :]
        bias[3 * HTILES + t] = seen[1, j, :, 0, :]
        bias[4 * HTILES + t] = seen[2, j, :, 1, :]
    bias[5 * HTILES] = jnp.full((TILES, 128), -jnp.inf, jnp.float32)
    kv[:, :, pl.ds(5 * HALF, SPAN - 5 * HALF), :] = jnp.zeros((2, 2, SPAN - 5 * HALF, WIDTH), jnp.bfloat16)

    hand_on_early(0)
    start(far_q(0, CROSS))
    give(1, OWN)
    take_mate_kv(1)
    give(1, MATE)
    relay(0, 1)
    hand_on_late(0)
    relay(1, 0)
    start(far_q(1, FAR))
    hand_on_early(1)
    start(far_q(1, CROSS))
    hand_on_late(1)
    relay(1, 1)

    stacked = 2 * HALF

    def attend(index):
        n, local = lax.rem(index, 2), index // 2
        query_tile = jnp.where(local == 1, half, other_half) * HTILES
        for pair in (0, 1):
            lanes = pl.ds(128 * pair, PAIR)
            base = 64 * pair
            at = lax.broadcasted_iota(jnp.int32, (HALF, PAIR), 1)
            qp = q[index, :, lanes]
            heads = [jnp.where((at >= base + DH * m) & (at < base + DH * (m + 1)), qp, jnp.zeros_like(qp)) for m in (0, 1)]
            qs = jnp.concatenate(heads, axis=0)
            top[...] = jnp.full((stacked, 128), -jnp.inf, jnp.float32)

            def score(i, _):
                for kb in (0, 1):
                    at_key = pl.multiple_of(i * (2 * KEYS) + kb * KEYS, KEYS)
                    k = kv[n, 0, pl.ds(at_key, KEYS), lanes]
                    sc = lax.dot_general(qs, k, (((1,), (1,)), ((), ())), preferred_element_type=jnp.float32)
                    cols = []
                    for kt in (0, 1):
                        parts = [jnp.broadcast_to(bias[i * 4 + kb * 2 + kt, pl.ds(query_tile + r, 1), :], (TILE, 128)) for r in range(HTILES)]
                        cols.append(jnp.concatenate(parts * 2, axis=0))
                    sc = sc + jnp.concatenate(cols, axis=1)
                    scores[i * 2 + kb] = sc
                    top[...] = jnp.maximum(top[...], jnp.maximum(sc[:, :128], sc[:, 128:]))
                return 0

            lax.fori_loop(0, STEPS, score, 0)
            top[...] = jnp.broadcast_to(jnp.max(top[...], axis=1, keepdims=True), (stacked, 128))
            total[...] = jnp.zeros((stacked, 128), jnp.float32)
            acc[...] = jnp.zeros((stacked, PAIR), jnp.float32)

            def weigh(i, _):
                ws = []
                highest = jnp.concatenate([top[...]] * 2, axis=1)
                for kb in (0, 1):
                    w = jnp.exp2((scores[i * 2 + kb] - highest) * SCALE)
                    total[...] += w[:, :128] + w[:, 128:]
                    ws.append(w.astype(jnp.bfloat16))
                at_key = pl.multiple_of(i * (2 * KEYS), KEYS)
                acc[...] += jnp.dot(jnp.concatenate(ws, axis=1), kv[n, 1, pl.ds(at_key, 2 * KEYS), lanes],
                                    preferred_element_type=jnp.float32)
                return 0

            lax.fori_loop(0, STEPS, weigh, 0)
            sums = jnp.sum(total[...], axis=1, keepdims=True)
            o = acc[...] / sums
            o = jnp.where(at < base + DH, o[:HALF], o[HALF:])
            first = at[:, :128]
            stats = jnp.zeros((HALF, 128), jnp.float32) if pair == 0 else stat[index]
            for m in (0, 1):
                head = 2 * pair + m
                mine = pl.ds(m * HALF, HALF)
                stats = jnp.where(first == 2 * head, top[mine, :], stats)
                stats = jnp.where(first == 2 * head + 1, sums[m * HALF:(m + 1) * HALF], stats)
            stat[index] = stats

            def put(ref):
                value = o
                if pair == 1:
                    value = jnp.concatenate([
                        jnp.where(first < 64, ref[n, :, pl.ds(128, 128)].astype(jnp.float32), o[:, :128]), o[:, 128:]], axis=1)
                ref[n, :, lanes] = value.astype(ref.dtype)

            pl.when(local == 0)(lambda: put(part))
            pl.when(local == 1)(lambda: put(near))

    def back(n):
        return (remote(part.at[n], partial_in.at[n], back_send.at[0, n], back_recv.at[0, n], far[FAR]),
                remote(stat_out.at[n], stat_in.at[n], back_send.at[1, n], back_recv.at[1, n], far[FAR]))

    def take_far_q(n, which):
        remote(x_ref.at[0, :, columns(core, n)], q.at[n, rows(core_of[which])], far_send.at[n, which], far_recv.at[n, which],
               far[which]).wait_recv()

    def take_mate_q(n):
        remote(x_ref.at[0, :, columns(core, n)], q.at[2 + n, rows(other_core)], mate_send.at[1, n], mate_recv.at[1, n], mate).wait_recv()

    def unit(index, _):
        for n in (0, 1):
            @pl.when(index == n)
            def _():
                own_kv[n].wait()
                for block in (OWN, MATE):
                    for direction in (0, 1):
                        passing(1, n, block, direction).wait_recv()
                take_far_q(n, FAR)
                take_far_q(n, CROSS)

            @pl.when(index == 2 + n)
            def _():
                own_q[n].wait()
                take_mate_q(n)

        attend(index)
        for n in (0, 1):
            @pl.when(index == n)
            def _():
                stat_out[n] = jnp.transpose(stat[n])[:8]
                for copy in back(n):
                    copy.start()

        return 0

    lax.fori_loop(0, 4, unit, 0)

    keep = [pltpu.make_async_copy(fin.at[n, rows(core)], out_ref.at[:, columns(core, n)], local_sem.at[5 + n]) for n in (0, 1)]

    def send_home(n):
        return remote(fin.at[n, rows(other_core)], out_ref.at[:, columns(core, n)], fin_send.at[n], fin_recv.at[n], mate)

    for n in (0, 1):
        for copy in back(n):
            copy.wait_recv()
        theirs = jnp.transpose(jnp.concatenate([stat_in[n], jnp.zeros((120, HALF), jnp.float32)], axis=0))
        ours = stat[2 + n]
        at = lax.broadcasted_iota(jnp.int32, (HALF, WIDTH), 1)
        for head in range(4):
            top_theirs, top_ours = theirs[:, 2 * head:2 * head + 1], ours[:, 2 * head:2 * head + 1]
            highest = jnp.maximum(top_theirs, top_ours)
            by_theirs = theirs[:, 2 * head + 1:2 * head + 2] * jnp.exp2((top_theirs - highest) * SCALE)
            by_ours = ours[:, 2 * head + 1:2 * head + 2] * jnp.exp2((top_ours - highest) * SCALE)
            whole = by_theirs + by_ours
            share_theirs, share_ours = by_theirs / whole, by_ours / whole
            if head == 0:
                all_theirs = jnp.broadcast_to(share_theirs, (HALF, WIDTH))
                all_ours = jnp.broadcast_to(share_ours, (HALF, WIDTH))
            else:
                all_theirs = jnp.where(at >= head * DH, share_theirs, all_theirs)
                all_ours = jnp.where(at >= head * DH, share_ours, all_ours)
        fin[n] = (partial_in[n].astype(jnp.float32) * all_theirs + near[n] * all_ours).astype(jnp.bfloat16)
        send_home(n).start()
        keep[n].start()

    for n in (0, 1):
        remote(fin.at[n, rows(other_core)], out_ref.at[:, columns(other_core, n)], fin_send.at[n], fin_recv.at[n], mate).wait_recv()
        send_home(n).wait_send()
        keep[n].wait()
        for copy in back(n):
            copy.wait_send()
    for copy in copies:
        copy.wait_send()
    for n in (0, 1):
        for block in (OWN, MATE):
            for direction in (0, 1):
                for kind in (0, 1):
                    passing(kind, n, block, direction).wait_send()

    @pl.when(relaying)
    def _():
        for kind in (0, 1):
            for n in (0, 1):
                hop(kind, n).wait_send()


def body(qkv, tile_masks):
    x = jnp.transpose(qkv[0], (1, 0, 2))
    masks = jnp.transpose(tile_masks, (2, 3, 1, 0))
    dma = pltpu.SemaphoreType.DMA
    stacked = 2 * HALF
    out = pl.pallas_call(
        kernel,
        out_shape=jax.ShapeDtypeStruct((ROWS, x.shape[2]), jnp.bfloat16),
        in_specs=[pl.BlockSpec(memory_space=pl.ANY)] * 2,
        out_specs=pl.BlockSpec(memory_space=pl.ANY),
        scratch_shapes=[
            pltpu.VMEM((2, 2, SPAN, WIDTH), jnp.bfloat16),
            pltpu.VMEM((4, HALF, WIDTH), jnp.bfloat16),
            pltpu.VMEM((2, HALF, WIDTH), jnp.bfloat16),
            pltpu.VMEM((2, HALF, WIDTH), jnp.bfloat16),
            pltpu.VMEM((2, HALF, WIDTH), jnp.float32),
            pltpu.VMEM((2, HALF, WIDTH), jnp.bfloat16),
            pltpu.VMEM((4, HALF, 128), jnp.float32),
            pltpu.VMEM((2, 8, HALF), jnp.float32),
            pltpu.VMEM((2, 8, HALF), jnp.float32),
            pltpu.VMEM((2 * STEPS, stacked, KEYS), jnp.float32),
            pltpu.VMEM((stacked, 128), jnp.float32),
            pltpu.VMEM((stacked, 128), jnp.float32),
            pltpu.VMEM((stacked, PAIR), jnp.float32),
            pltpu.VMEM(masks.shape, jnp.int32),
            pltpu.VMEM((3, TILES, TILES, 2, 128), jnp.float32),
            pltpu.VMEM((4 * STEPS, TILES, 128), jnp.float32),
            pltpu.VMEM((2, 2, ROWS, WIDTH), jnp.bfloat16),
            dma((7,)),
            dma((2, 2)), dma((2, 2)),
            dma((2, 2)), dma((2, 2)),
            dma((2, 2, 2)), dma((2, 2, 2)),
            dma((2, 2, 2)), dma((2, 2, 2)),
            dma((2, 2)), dma((2, 2)),
            dma((2, 2)), dma((2, 2)),
            dma((2,)), dma((2,)),
        ],
        compiler_params=pltpu.CompilerParams(collective_id=1, has_side_effects=True, vmem_limit_bytes=48 * 2**20),
        name="orbit_attention",
    )(x, masks)
    return out[None]


def solution(mesh):
    placed = (P("video", "head", None, None), P())
    return jax.shard_map(
        body, mesh=mesh, in_specs=placed, out_specs=P("video", "head", None), check_vma=False
    )
```

time: 378 us -> 178 us (0.47)
  the two profiles are of different devices: /device:TPU:152 before, /device:TPU:65 now
where the time goes in v2:
time: 178 us
  Pallas kernels  174 us (98%)
  local copies, waits for them, and re-layouts  3.06 us (2%)
    pallas_call x1, Pallas kernels, body(): pl.pallas_call(kernel, out_shape=jax.ShapeDtypeStruct((ROWS, x.shape[2]),...  174 us

profile of v2, /device:TPU:65, one launch (start us, length us, event | category | flops | bytes accessed | tf_op | source)
XLA Modules:
  0.0 177.5 jit_solution(14397715130107876087)
XLA Ops:
  0.0 0.0 copy-start
  0.0 1.5 copy-done
  1.5 0.0 copy-start.1
  1.5 0.8 copy-done.1
  2.2 174.4 %orbit_attention.1 = bf16[192,1536]{1,0:T(8,128)(2,1)S(1)} custom-call(bf16[3,192,1536]{2,1,0:T(8,128)(2,1)S(1)} %bitcast.6, s32[6,6,2,128]{3,2,1,0:T(2,128)S(1)} %bitcast.7), custom_call_target="tpu_custom_call" | custom-call | tf_op jit(solution)/shard_map/orbit_attention/pallas_call | solution.py:383
  176.7 0.8 copy.4
Async XLA Ops:
  0.0 1.5 copy-start
  1.5 0.8 copy-start.1

commit v3 on v2

v3 whole, which is shorter than its diff:
```python
import jax
import jax.numpy as jnp
from jax import lax
from jax.experimental import pallas as pl
from jax.experimental.pallas import tpu as pltpu
from jax.sharding import PartitionSpec as P

MESH = pl.DeviceIdType.MESH
DH = 96
TILE = 128
ROWS = 192
HALF = 384
TILES = 6
HTILES = HALF // TILE
WIDTH = 384
PAIR = 256
KEYS = 256
SPAN = 2048
STEPS = 4
SCALE = DH ** (-0.5) * 1.4426950408889634
OWN, MATE = 0, 1
FAR, CROSS = 0, 1
PLANE = 16
SIDE = 4
EDGE = (0, PLANE - 1)


def kernel(x_ref, masks_ref, out_ref, kv, q, part, partial_in, near, fin, stat, stat_out, stat_in, stack, scores, top, total, acc,
           masks, seen, bias, held, landed, local_sem, mate_send, mate_recv, far_send, far_recv, nb_send, nb_recv, fw_send, fw_recv,
           leap_send, hop_send, hop_recv, land_send, land_recv, back_send, back_recv, fin_send, fin_recv):
    video = lax.axis_index("video")
    group = lax.axis_index("head")
    videos = lax.axis_size("video")
    half, core = group // 2, lax.rem(group, 2)
    other_half, other_core = 1 - half, 1 - core
    up = lax.rem(video + 1, videos)
    down = lax.rem(video + videos - 1, videos)
    planes = videos // PLANE
    plane, column = video // PLANE, lax.rem(video, PLANE)
    across, row = column // SIDE, lax.rem(column, SIDE)

    mate = {"video": video, "head": half * 2 + other_core}
    far = ({"video": video, "head": other_half * 2 + core}, {"video": video, "head": other_half * 2 + other_core})

    def along(direction):
        return {"video": (down, up)[direction], "head": group}

    def at_column(level, col):
        return {"video": lax.rem(level + planes, planes) * PLANE + col, "head": group}

    def columns(of_core, n):
        return pl.ds(pl.multiple_of((of_core * 2 + n) * WIDTH, 128), WIDTH)

    def rows(of_core, slot=0):
        return pl.ds(pl.multiple_of(slot * HALF + of_core * ROWS, 64), ROWS)

    both = pl.ds(1, 2)
    core_of = (core, other_core)

    def remote(src, dst, send, recv, to):
        return pltpu.make_async_remote_copy(
            src_ref=src, dst_ref=dst, send_sem=send, recv_sem=recv, device_id=to, device_id_type=MESH)

    copies = []

    def start(copy):
        copy.start()
        copies.append(copy)

    get_masks = pltpu.make_async_copy(masks_ref, masks, local_sem.at[0])
    own_kv = [pltpu.make_async_copy(x_ref.at[both, :, columns(core, n)], kv.at[n, :, rows(core)], local_sem.at[1 + n]) for n in (0, 1)]
    own_q = [pltpu.make_async_copy(x_ref.at[0, :, columns(core, n)], q.at[2 * n + 1, rows(core)], local_sem.at[3 + n]) for n in (0, 1)]
    get_masks.start()
    for copy in own_kv + own_q:
        copy.start()

    barrier = pltpu.get_barrier_semaphore()

    def greet(to):
        pl.semaphore_signal(barrier, inc=1, device_id=to, device_id_type=MESH)

    for to in (*far, mate, along(0), along(1)):
        greet(to)

    upward = row >= SIDE // 2
    outer = (row == 0) | (row == SIDE - 1)
    origin = row + jnp.where(upward, (SIDE - 1) * SIDE, 0)
    leaving = column != origin
    ahead = jnp.where(upward, 1, -1)
    next_plane = at_column(plane + ahead, column)
    sink = at_column(plane, jnp.where(upward, EDGE[0], EDGE[1]))
    pl.when(leaving)(lambda: greet(at_column(plane, origin)))
    greet(at_column(plane - ahead, column))
    for direction in (0, 1):
        @pl.when(column == EDGE[1 - direction])
        def _():
            for place in range(SIDE):
                for line in (2 * direction, 2 * direction + 1):
                    greet(at_column(plane, place * SIDE + line))

    expected = jnp.where(leaving, 7, 6 + SIDE)
    pl.semaphore_wait(barrier, expected)

    def mate_kv(n):
        return remote(x_ref.at[both, :, columns(other_core, n)], kv.at[n, :, rows(core)], mate_send.at[0, n], mate_recv.at[0, n], mate)

    def mate_q(n):
        return remote(x_ref.at[0, :, columns(other_core, n)], q.at[2 * n + 1, rows(core)], mate_send.at[1, n], mate_recv.at[1, n], mate)

    def far_q(n, which, part=None):
        src, dst = x_ref.at[0, :, columns(core_of[which], n)], q.at[2 * n, rows(core)]
        if part is not None:
            src, dst = src.at[pl.ds(part * (ROWS // 2), ROWS // 2)], dst.at[pl.ds(part * (ROWS // 2), ROWS // 2)]
        return remote(src, dst, far_send.at[n, which], far_recv.at[n, which], far[which])

    slots = ((1, 3), (2, 4))

    def source_of(kind, n, block, direction):
        if kind:
            return kv.at[n, :, rows(core_of[block], slots[0][direction])]
        if block == OWN:
            return x_ref.at[both, :, columns(core, n)]
        return kv.at[n, :, rows(other_core)]

    def sems(kind, n, block, direction):
        send, recv = ((nb_send, nb_recv), (fw_send, fw_recv))[kind]
        return send.at[direction, n, block], recv.at[direction, n, block]

    def target_of(kind, n, block, direction):
        return kv.at[n, :, rows(core_of[block], slots[kind][direction])]

    def passing(kind, n, block, direction):
        return remote(source_of(kind, n, block, direction), target_of(kind, n, block, direction),
                      *sems(kind, n, block, direction), along(direction))

    def step(kind, n, block, direction):
        pl.when(column != EDGE[direction])(passing(kind, n, block, direction).start)

    def leap(n, block):
        @pl.when(column == origin)
        def _():
            for which in (0, 1):
                place = block * 2 + which
                src = source_of(0, n, block, 0).at[which]
                pl.when(across == place)(
                    remote(src, landed.at[n], leap_send.at[n, block], land_recv.at[n], next_plane).start)
                pl.when(across != place)(
                    remote(src, held.at[n], leap_send.at[n, block], hop_recv.at[n], at_column(plane, place * SIDE + row)).start)

    def hop(n):
        return remote(held.at[n], landed.at[n], hop_send.at[n], land_recv.at[n], next_plane)

    def land(n, kind):
        block, which = across // 2, lax.rem(across, 2)
        slot = jnp.where(upward, slots[kind][1], slots[kind][0])
        recv = (nb_recv, fw_recv)[kind].at[upward.astype(jnp.int32), n, block]
        return remote(landed.at[n], kv.at[n, which, rows(lax.rem(core + block, 2), slot)], land_send.at[n], recv, sink)

    def relay(n):
        @pl.when(leaving)
        def _():
            remote(held.at[n], held.at[n], hop_send.at[n], hop_recv.at[n], next_plane).wait_recv()
            hop(n).start()

    def arrive(n, kind):
        @pl.when(outer if kind == 0 else jnp.logical_not(outer))
        def _():
            hop(n).wait_recv()
            land(n, kind).start()

    def hand_on(n, direction):
        for block in (OWN, MATE):
            passing(0, n, block, direction).wait_recv()
            step(1, n, block, direction)

    def hand_on_early(n, direction):
        pl.when(column != EDGE[1 - direction])(lambda: hand_on(n, direction))

    def hand_on_late(n):
        for direction in (0, 1):
            pl.when(column == EDGE[1 - direction])(lambda direction=direction: hand_on(n, direction))

    def give(n, block):
        for direction in (0, 1):
            step(0, n, block, direction)

    def take_mate_kv(n):
        remote(x_ref.at[both, :, columns(core, n)], kv.at[n, :, rows(other_core)], mate_send.at[0, n], mate_recv.at[0, n], mate).wait_recv()

    start(mate_kv(0))
    leap(0, OWN)
    give(0, OWN)
    far_q(0, FAR, 0).start()
    start(mate_kv(1))
    start(mate_q(0))
    start(mate_q(1))
    take_mate_kv(0)
    leap(0, MATE)
    give(0, MATE)
    leap(1, OWN)
    take_mate_kv(1)
    leap(1, MATE)
    relay(0)
    relay(1)
    far_q(0, FAR, 1).start()
    copies.append(far_q(0, FAR))

    get_masks.wait()
    lane = lax.broadcasted_iota(jnp.int32, (TILES, TILES, 2, 128), 3)
    for back in (0, 1, 2):
        who = lax.rem(video + videos - back, videos)
        value = jnp.sum(jnp.where(lane == who, masks[...].astype(jnp.float32), 0.0), axis=3, keepdims=True)
        seen[back] = jnp.broadcast_to(jnp.where(value > 0.5, 0.0, -jnp.inf), (TILES, TILES, 2, 128))
    for t in range(HTILES):
        j = half * HTILES + t
        bias[t] = jnp.zeros((TILES, 128), jnp.float32)
        bias[HTILES + t] = seen[0, :, j, 0, :]
        bias[2 * HTILES + t] = seen[0, :, j, 1, :]
        bias[3 * HTILES + t] = seen[1, j, :, 0, :]
        bias[4 * HTILES + t] = seen[2, j, :, 1, :]
    bias[5 * HTILES] = jnp.full((TILES, 128), -jnp.inf, jnp.float32)
    kv[:, :, pl.ds(5 * HALF, SPAN - 5 * HALF), :] = jnp.zeros((2, 2, SPAN - 5 * HALF, WIDTH), jnp.bfloat16)

    start(far_q(0, CROSS))
    hand_on_early(0, 0)
    hand_on_early(0, 1)
    start(far_q(1, FAR))
    arrive(0, 0)
    arrive(0, 1)
    give(1, OWN)
    give(1, MATE)
    start(far_q(1, CROSS))
    hand_on_late(0)
    hand_on_early(1, 0)
    hand_on_early(1, 1)
    arrive(1, 0)

    stacked = 2 * HALF

    def attend(index):
        n, local = index // 2, lax.rem(index, 2)
        query_tile = jnp.where(local == 1, half, other_half) * HTILES
        at = lax.broadcasted_iota(jnp.int32, (HALF, PAIR), 1)
        lanes = [pl.ds(128 * pair, PAIR) for pair in (0, 1)]
        base = (0, 64)
        for pair in (0, 1):
            qp = q[index, :, lanes[pair]]
            for m in (0, 1):
                low = base[pair] + DH * m
                stack[pair, pl.ds(m * HALF, HALF), :] = jnp.where((at >= low) & (at < low + DH), qp, jnp.zeros_like(qp))
            top[pair] = jnp.full((stacked, 128), -jnp.inf, jnp.float32)
            total[pair] = jnp.zeros((stacked, 128), jnp.float32)
            acc[pair] = jnp.zeros((stacked, PAIR), jnp.float32)

        def score(pair, i):
            for kb in (0, 1):
                at_key = pl.multiple_of(i * (2 * KEYS) + kb * KEYS, KEYS)
                k = kv[n, 0, pl.ds(at_key, KEYS), lanes[pair]]
                sc = lax.dot_general(stack[pair], k, (((1,), (1,)), ((), ())), preferred_element_type=jnp.float32)
                cols = []
                for kt in (0, 1):
                    parts = [jnp.broadcast_to(bias[i * 4 + kb * 2 + kt, pl.ds(query_tile + r, 1), :], (TILE, 128)) for r in range(HTILES)]
                    cols.append(jnp.concatenate(parts * 2, axis=0))
                sc = sc + jnp.concatenate(cols, axis=1)
                scores[pair, i * 2 + kb] = sc
                top[pair] = jnp.maximum(top[pair], jnp.maximum(sc[:, :128], sc[:, 128:]))

        def weigh(pair, i):
            ws = []
            highest = jnp.concatenate([top[pair]] * 2, axis=1)
            for kb in (0, 1):
                w = jnp.exp2((scores[pair, i * 2 + kb] - highest) * SCALE)
                total[pair] += w[:, :128] + w[:, 128:]
                ws.append(w.astype(jnp.bfloat16))
            at_key = pl.multiple_of(i * (2 * KEYS), KEYS)
            acc[pair] += jnp.dot(jnp.concatenate(ws, axis=1), kv[n, 1, pl.ds(at_key, 2 * KEYS), lanes[pair]],
                                 preferred_element_type=jnp.float32)

        def highest_of(pair):
            top[pair] = jnp.broadcast_to(jnp.max(top[pair], axis=1, keepdims=True), (stacked, 128))

        def finish(pair):
            sums = jnp.sum(total[pair], axis=1, keepdims=True)
            o = acc[pair] / sums
            o = jnp.where(at < base[pair] + DH, o[:HALF], o[HALF:])
            first = at[:, :128]
            stats = jnp.zeros((HALF, 128), jnp.float32) if pair == 0 else stat[index]
            for m in (0, 1):
                head = 2 * pair + m
                stats = jnp.where(first == 2 * head, top[pair, pl.ds(m * HALF, HALF), :], stats)
                stats = jnp.where(first == 2 * head + 1, sums[m * HALF:(m + 1) * HALF], stats)
            stat[index] = stats

            def put(ref):
                value = o
                if pair == 1:
                    value = jnp.concatenate([
                        jnp.where(first < 64, ref[n, :, pl.ds(128, 128)].astype(jnp.float32), o[:, :128]), o[:, 128:]], axis=1)
                ref[n, :, lanes[pair]] = value.astype(ref.dtype)

            pl.when(local == 0)(lambda: put(part))
            pl.when(local == 1)(lambda: put(near))

        @pl.loop(0, STEPS)
        def _(i):
            score(0, i)

        highest_of(0)

        @pl.loop(0, STEPS)
        def _(i):
            weigh(0, i)
            score(1, i)

        highest_of(1)
        finish(0)

        @pl.loop(0, STEPS)
        def _(i):
            weigh(1, i)

        finish(1)

    def back(n):
        return (remote(part.at[n], partial_in.at[n], back_send.at[0, n], back_recv.at[0, n], far[FAR]),
                remote(stat_out.at[n], stat_in.at[n], back_send.at[1, n], back_recv.at[1, n], far[FAR]))

    def take_far_q(n, which):
        remote(x_ref.at[0, :, columns(core, n)], q.at[2 * n, rows(core_of[which])], far_send.at[n, which], far_recv.at[n, which],
               far[which]).wait_recv()

    def take_mate_q(n):
        remote(x_ref.at[0, :, columns(core, n)], q.at[2 * n + 1, rows(other_core)], mate_send.at[1, n], mate_recv.at[1, n], mate).wait_recv()

    def unit(index, _):
        for n in (0, 1):
            @pl.when(index == 2 * n)
            def _():
                own_kv[n].wait()
                for block in (OWN, MATE):
                    for direction in (0, 1):
                        passing(1, n, block, direction).wait_recv()
                take_far_q(n, FAR)
                take_far_q(n, CROSS)

            @pl.when(index == 2 * n + 1)
            def _():
                own_q[n].wait()
                take_mate_q(n)

        attend(index)
        for n in (0, 1):
            @pl.when(index == 2 * n)
            def _():
                stat_out[n] = jnp.transpose(stat[2 * n])[:8]
                for copy in back(n):
                    copy.start()
                if n == 0:
                    hand_on_late(1)
                    arrive(1, 1)

        return 0

    lax.fori_loop(0, 4, unit, 0)

    keep = [pltpu.make_async_copy(fin.at[n, rows(core)], out_ref.at[:, columns(core, n)], local_sem.at[5 + n]) for n in (0, 1)]

    def send_home(n):
        return remote(fin.at[n, rows(other_core)], out_ref.at[:, columns(core, n)], fin_send.at[n], fin_recv.at[n], mate)

    for n in (0, 1):
        for copy in back(n):
            copy.wait_recv()
        theirs = jnp.transpose(jnp.concatenate([stat_in[n], jnp.zeros((120, HALF), jnp.float32)], axis=0))
        ours = stat[2 * n + 1]
        at = lax.broadcasted_iota(jnp.int32, (HALF, WIDTH), 1)
        for head in range(4):
            top_theirs, top_ours = theirs[:, 2 * head:2 * head + 1], ours[:, 2 * head:2 * head + 1]
            highest = jnp.maximum(top_theirs, top_ours)
            by_theirs = theirs[:, 2 * head + 1:2 * head + 2] * jnp.exp2((top_theirs - highest) * SCALE)
            by_ours = ours[:, 2 * head + 1:2 * head + 2] * jnp.exp2((top_ours - highest) * SCALE)
            whole = by_theirs + by_ours
            share_theirs, share_ours = by_theirs / whole, by_ours / whole
            if head == 0:
                all_theirs = jnp.broadcast_to(share_theirs, (HALF, WIDTH))
                all_ours = jnp.broadcast_to(share_ours, (HALF, WIDTH))
            else:
                all_theirs = jnp.where(at >= head * DH, share_theirs, all_theirs)
                all_ours = jnp.where(at >= head * DH, share_ours, all_ours)
        fin[n] = (partial_in[n].astype(jnp.float32) * all_theirs + near[n] * all_ours).astype(jnp.bfloat16)
        send_home(n).start()
        keep[n].start()

    for n in (0, 1):
        remote(fin.at[n, rows(other_core)], out_ref.at[:, columns(other_core, n)], fin_send.at[n], fin_recv.at[n], mate).wait_recv()
        send_home(n).wait_send()
        keep[n].wait()
        for copy in back(n):
            copy.wait_send()
    for copy in copies:
        copy.wait_send()
    for n in (0, 1):
        for block in (OWN, MATE):
            for direction in (0, 1):
                for kind in (0, 1):
                    pl.when(column != EDGE[direction])(passing(kind, n, block, direction).wait_send)
            pl.when(column == origin)(
                remote(kv.at[n, :, rows(core)], kv.at[n, :, rows(core)], leap_send.at[n, block], nb_recv.at[0, n, block], mate).wait_send)
        pl.when(leaving)(hop(n).wait_send)
        land(n, 0).wait_send()


def body(qkv, tile_masks):
    x = jnp.transpose(qkv[0], (1, 0, 2))
    masks = jnp.transpose(tile_masks, (2, 3, 1, 0))
    dma = pltpu.SemaphoreType.DMA
    stacked = 2 * HALF
    out = pl.pallas_call(
        kernel,
        out_shape=jax.ShapeDtypeStruct((ROWS, x.shape[2]), jnp.bfloat16),
        in_specs=[pl.BlockSpec(memory_space=pl.ANY)] * 2,
        out_specs=pl.BlockSpec(memory_space=pl.ANY),
        scratch_shapes=[
            pltpu.VMEM((2, 2, SPAN, WIDTH), jnp.bfloat16),
            pltpu.VMEM((4, HALF, WIDTH), jnp.bfloat16),
            pltpu.VMEM((2, HALF, WIDTH), jnp.bfloat16),
            pltpu.VMEM((2, HALF, WIDTH), jnp.bfloat16),
            pltpu.VMEM((2, HALF, WIDTH), jnp.float32),
            pltpu.VMEM((2, HALF, WIDTH), jnp.bfloat16),
            pltpu.VMEM((4, HALF, 128), jnp.float32),
            pltpu.VMEM((2, 8, HALF), jnp.float32),
            pltpu.VMEM((2, 8, HALF), jnp.float32),
            pltpu.VMEM((2, stacked, PAIR), jnp.bfloat16),
            pltpu.VMEM((2, 2 * STEPS, stacked, KEYS), jnp.float32),
            pltpu.VMEM((2, stacked, 128), jnp.float32),
            pltpu.VMEM((2, stacked, 128), jnp.float32),
            pltpu.VMEM((2, stacked, PAIR), jnp.float32),
            pltpu.VMEM(masks.shape, jnp.int32),
            pltpu.VMEM((3, TILES, TILES, 2, 128), jnp.float32),
            pltpu.VMEM((4 * STEPS, TILES, 128), jnp.float32),
            pltpu.VMEM((2, ROWS, WIDTH), jnp.bfloat16),
            pltpu.VMEM((2, ROWS, WIDTH), jnp.bfloat16),
            dma((7,)),
            dma((2, 2)), dma((2, 2)),
            dma((2, 2)), dma((2, 2)),
            dma((2, 2, 2)), dma((2, 2, 2)),
            dma((2, 2, 2)), dma((2, 2, 2)),
            dma((2, 2)),
            dma((2,)), dma((2,)),
            dma((2,)), dma((2,)),
            dma((2, 2)), dma((2, 2)),
            dma((2,)), dma((2,)),
        ],
        compiler_params=pltpu.CompilerParams(collective_id=1, has_side_effects=True, vmem_limit_bytes=60 * 2**20),
        name="orbit_attention",
    )(x, masks)
    return out[None]


def solution(mesh):
    placed = (P("video", "head", None, None), P())
    return jax.shard_map(
        body, mesh=mesh, in_specs=placed, out_specs=P("video", "head", None), check_vma=False
    )
```

time: 178 us -> 144 us (0.81)
  the two profiles are of different devices: /device:TPU:65 before, /device:TPU:1 now
where the time goes in v3:
time: 144 us
  Pallas kernels  142 us (99%)
  local copies, waits for them, and re-layouts  1.92 us (1%)
    pallas_call x1, Pallas kernels, body(): pl.pallas_call(kernel, out_shape=jax.ShapeDtypeStruct((ROWS, x.shape[2]),...  142 us

profile of v3, /device:TPU:1, one launch (start us, length us, event | category | flops | bytes accessed | tf_op | source)
XLA Modules:
  0.0 143.5 jit_solution(3720050881559075427)
XLA Ops:
  0.0 141.6 %orbit_attention.1 = bf16[192,1536]{1,0:T(8,128)(2,1)} custom-call(bf16[3,192,1536]{2,1,0:T(8,128)(2,1)} %bitcast.6, s32[6,6,2,128]{3,2,1,0:T(2,128)} %bitcast.7), custom_call_target="tpu_custom_call" | custom-call | tf_op jit(solution)/shard_map/orbit_attention/pallas_call | solution.py:418
  141.6 1.9 %copy.4 = bf16[1,192,1536]{2,1,0:T(8,128)(2,1)} copy(bf16[1,192,1536]{2,1,0:T(8,128)(2,1)} %bitcast.5) | data formatting | bytes 1179648

commit v4 on v3

--- a/solution.py
+++ b/solution.py
@@ -22,10 +22,11 @@
 FAR, CROSS = 0, 1
 PLANE = 16
 SIDE = 4
+SLOW = (PLANE - SIDE, SIDE - 1)
 EDGE = (0, PLANE - 1)
 
 
-def kernel(x_ref, masks_ref, out_ref, kv, q, part, partial_in, near, fin, stat, stat_out, stat_in, stack, scores, top, total, acc,
+def kernel(x_ref, masks_ref, out_ref, kv, q, part, partial_in, near, fin, stat, stat_out, stat_in, shares, stack, scores, top, total, acc,
            masks, seen, bias, held, landed, local_sem, mate_send, mate_recv, far_send, far_recv, nb_send, nb_recv, fw_send, fw_recv,
            leap_send, hop_send, hop_recv, land_send, land_recv, back_send, back_recv, fin_send, fin_recv):
     video = lax.axis_index("video")
@@ -89,6 +90,7 @@
     ahead = jnp.where(upward, 1, -1)
     next_plane = at_column(plane + ahead, column)
     sink = at_column(plane, jnp.where(upward, EDGE[0], EDGE[1]))
+    wrapped = jnp.where(upward, plane == 0, plane == planes - 1)
     pl.when(leaving)(lambda: greet(at_column(plane, origin)))
     greet(at_column(plane - ahead, column))
     for direction in (0, 1):
@@ -173,12 +175,16 @@
             passing(0, n, block, direction).wait_recv()
             step(1, n, block, direction)
 
+    def is_late(n, direction):
+        late = column == EDGE[1 - direction]
+        return late | (column == SLOW[direction]) if n else late
+
     def hand_on_early(n, direction):
-        pl.when(column != EDGE[1 - direction])(lambda: hand_on(n, direction))
+        pl.when(jnp.logical_not(is_late(n, direction)))(lambda: hand_on(n, direction))
 
     def hand_on_late(n):
         for direction in (0, 1):
-            pl.when(column == EDGE[1 - direction])(lambda direction=direction: hand_on(n, direction))
+            pl.when(is_late(n, direction))(lambda direction=direction: hand_on(n, direction))
 
     def give(n, block):
         for direction in (0, 1):
@@ -233,7 +239,7 @@
     hand_on_late(0)
     hand_on_early(1, 0)
     hand_on_early(1, 1)
-    arrive(1, 0)
+    pl.when(jnp.logical_not(wrapped))(lambda: arrive(1, 0))
 
     stacked = 2 * HALF
 
@@ -340,6 +346,8 @@
                 for block in (OWN, MATE):
                     for direction in (0, 1):
                         passing(1, n, block, direction).wait_recv()
+                if n == 0:
+                    arrive(1, 1)
                 take_far_q(n, FAR)
                 take_far_q(n, CROSS)
 
@@ -356,8 +364,8 @@
                 for copy in back(n):
                     copy.start()
                 if n == 0:
+                    pl.when(wrapped)(lambda: arrive(1, 0))
                     hand_on_late(1)
-                    arrive(1, 1)
 
         return 0
 
@@ -371,24 +379,27 @@
     for n in (0, 1):
         for copy in back(n):
             copy.wait_recv()
-        theirs = jnp.transpose(jnp.concatenate([stat_in[n], jnp.zeros((120, HALF), jnp.float32)], axis=0))
-        ours = stat[2 * n + 1]
-        at = lax.broadcasted_iota(jnp.int32, (HALF, WIDTH), 1)
-        for head in range(4):
-            top_theirs, top_ours = theirs[:, 2 * head:2 * head + 1], ours[:, 2 * head:2 * head + 1]
-            highest = jnp.maximum(top_theirs, top_ours)
-            by_theirs = theirs[:, 2 * head + 1:2 * head + 2] * jnp.exp2((top_theirs - highest) * SCALE)
-            by_ours = ours[:, 2 * head + 1:2 * head + 2] * jnp.exp2((top_ours - highest) * SCALE)
-            whole = by_theirs + by_ours
-            share_theirs, share_ours = by_theirs / whole, by_ours / whole
-            if head == 0:
-                all_theirs = jnp.broadcast_to(share_theirs, (HALF, WIDTH))
-                all_ours = jnp.broadcast_to(share_ours, (HALF, WIDTH))
-            else:
-                all_theirs = jnp.where(at >= head * DH, share_theirs, all_theirs)
-                all_ours = jnp.where(at >= head * DH, share_ours, all_ours)
-        fin[n] = (partial_in[n].astype(jnp.float32) * all_theirs + near[n] * all_ours).astype(jnp.bfloat16)
-        send_home(n).start()
+        shares[...] = jnp.transpose(jnp.concatenate([stat_in[n], jnp.zeros((120, HALF), jnp.float32)], axis=0))
+        for whose in (other_core, core):
+            block = rows(whose)
+            theirs, ours = shares[block, :], stat[2 * n + 1, block, :]
+            at = lax.broadcasted_iota(jnp.int32, (ROWS, WIDTH), 1)
+            for head in range(4):
+                top_theirs, top_ours = theirs[:, 2 * head:2 * head + 1], ours[:, 2 * head:2 * head + 1]
+                highest = jnp.maximum(top_theirs, top_ours)
+                by_theirs = theirs[:, 2 * head + 1:2 * head + 2] * jnp.exp2((top_theirs - highest) * SCALE)
+                by_ours = ours[:, 2 * head + 1:2 * head + 2] * jnp.exp2((top_ours - highest) * SCALE)
+                whole = by_theirs + by_ours
+                share_theirs, share_ours = by_theirs / whole, by_ours / whole
+                if head == 0:
+                    all_theirs = jnp.broadcast_to(share_theirs, (ROWS, WIDTH))
+                    all_ours = jnp.broadcast_to(share_ours, (ROWS, WIDTH))
+                else:
+                    all_theirs = jnp.where(at >= head * DH, share_theirs, all_theirs)
+                    all_ours = jnp.where(at >= head * DH, share_ours, all_ours)
+            fin[n, block, :] = (partial_in[n, block, :].astype(jnp.float32) * all_theirs + near[n, block, :] * all_ours).astype(jnp.bfloat16)
+            if whose is other_core:
+                send_home(n).start()
         keep[n].start()
 
     for n in (0, 1):
@@ -430,6 +441,7 @@
             pltpu.VMEM((4, HALF, 128), jnp.float32),
             pltpu.VMEM((2, 8, HALF), jnp.float32),
             pltpu.VMEM((2, 8, HALF), jnp.float32),
+            pltpu.VMEM((HALF, 128), jnp.float32),
             pltpu.VMEM((2, stacked, PAIR), jnp.bfloat16),
             pltpu.VMEM((2, 2 * STEPS, stacked, KEYS), jnp.float32),
             pltpu.VMEM((2, stacked, 128), jnp.float32),

time: 144 us -> 144 us (level)
  the two profiles are of different devices: /device:TPU:1 before, /device:TPU:61 now
where the time goes in v4:
time: 144 us; the launch traced here: 143 us
  Pallas kernels  142 us (99%)
  local copies, waits for them, and re-layouts  1.92 us (1%)
    pallas_call x1, Pallas kernels, body(): pl.pallas_call(kernel, out_shape=jax.ShapeDtypeStruct((ROWS, x.shape[2]),...  142 us

profile of v4, /device:TPU:61, one launch (start us, length us, event | category | flops | bytes accessed | tf_op | source)
XLA Modules:
  0.0 143.5 jit_solution(1797478033510792822)
XLA Ops:
  0.0 141.6 %orbit_attention.1 = bf16[192,1536]{1,0:T(8,128)(2,1)} custom-call(bf16[3,192,1536]{2,1,0:T(8,128)(2,1)} %bitcast.6, s32[6,6,2,128]{3,2,1,0:T(2,128)} %bitcast.7), custom_call_target="tpu_custom_call" | custom-call | tf_op jit(solution)/shard_map/orbit_attention/pallas_call | solution.py:429
  141.6 1.9 %copy.4 = bf16[1,192,1536]{2,1,0:T(8,128)(2,1)} copy(bf16[1,192,1536]{2,1,0:T(8,128)(2,1)} %bitcast.5) | data formatting | bytes 1179648

commit v5 on v4

--- a/solution.py
+++ b/solution.py
@@ -230,14 +230,20 @@
     start(far_q(0, CROSS))
     hand_on_early(0, 0)
     hand_on_early(0, 1)
-    start(far_q(1, FAR))
+    at_corner = (column == EDGE[0]) | (column == EDGE[1])
+    copies.append(far_q(1, FAR))
+    copies.append(far_q(1, CROSS))
+    far_q(1, FAR, 0).start()
+    pl.when(outer)(far_q(1, FAR, 1).start)
     arrive(0, 0)
     arrive(0, 1)
     give(1, OWN)
     give(1, MATE)
-    start(far_q(1, CROSS))
+    pl.when(at_corner)(far_q(1, CROSS).start)
     hand_on_late(0)
     hand_on_early(1, 0)
+    pl.when(jnp.logical_not(outer))(far_q(1, FAR, 1).start)
+    pl.when(jnp.logical_not(at_corner))(far_q(1, CROSS).start)
     hand_on_early(1, 1)
     pl.when(jnp.logical_not(wrapped))(lambda: arrive(1, 0))
 

time: 144 us -> 144 us (level)
  the two profiles are of different devices: /device:TPU:61 before, /device:TPU:29 now
where the time goes in v5:
time: 144 us
  Pallas kernels  142 us (99%)
  local copies, waits for them, and re-layouts  1.92 us (1%)
    pallas_call x1, Pallas kernels, body(): pl.pallas_call(kernel, out_shape=jax.ShapeDtypeStruct((ROWS, x.shape[2]),...  142 us

profile of v5, /device:TPU:29, one launch (start us, length us, event | category | flops | bytes accessed | tf_op | source)
XLA Modules:
  0.0 143.9 jit_solution(16386323349228823157)
XLA Ops:
  0.0 141.9 %orbit_attention.1 = bf16[192,1536]{1,0:T(8,128)(2,1)} custom-call(bf16[3,192,1536]{2,1,0:T(8,128)(2,1)} %bitcast.6, s32[6,6,2,128]{3,2,1,0:T(2,128)} %bitcast.7), custom_call_target="tpu_custom_call" | custom-call | tf_op jit(solution)/shard_map/orbit_attention/pallas_call | solution.py:435
  141.9 1.9 %copy.4 = bf16[1,192,1536]{2,1,0:T(8,128)(2,1)} copy(bf16[1,192,1536]{2,1,0:T(8,128)(2,1)} %bitcast.5) | data formatting | bytes 1179648

commit v6 on v4

--- a/solution.py
+++ b/solution.py
@@ -90,7 +90,6 @@
     ahead = jnp.where(upward, 1, -1)
     next_plane = at_column(plane + ahead, column)
     sink = at_column(plane, jnp.where(upward, EDGE[0], EDGE[1]))
-    wrapped = jnp.where(upward, plane == 0, plane == planes - 1)
     pl.when(leaving)(lambda: greet(at_column(plane, origin)))
     greet(at_column(plane - ahead, column))
     for direction in (0, 1):
@@ -239,7 +238,7 @@
     hand_on_late(0)
     hand_on_early(1, 0)
     hand_on_early(1, 1)
-    pl.when(jnp.logical_not(wrapped))(lambda: arrive(1, 0))
+    arrive(1, 0)
 
     stacked = 2 * HALF
 
@@ -346,8 +345,6 @@
                 for block in (OWN, MATE):
                     for direction in (0, 1):
                         passing(1, n, block, direction).wait_recv()
-                if n == 0:
-                    arrive(1, 1)
                 take_far_q(n, FAR)
                 take_far_q(n, CROSS)
 
@@ -364,8 +361,8 @@
                 for copy in back(n):
                     copy.start()
                 if n == 0:
-                    pl.when(wrapped)(lambda: arrive(1, 0))
                     hand_on_late(1)
+                    arrive(1, 1)
 
         return 0
 

time: 144 us -> 144 us (level)
  the two profiles are of different devices: /device:TPU:61 before, /device:TPU:1 now
where the time goes in v6:
time: 144 us; the launch traced here: 143 us
  Pallas kernels  141 us (98%)
  local copies, waits for them, and re-layouts  1.92 us (1%)
    pallas_call x1, Pallas kernels, body(): pl.pallas_call(kernel, out_shape=jax.ShapeDtypeStruct((ROWS, x.shape[2]),...  141 us

profile of v6, /device:TPU:1, one launch (start us, length us, event | category | flops | bytes accessed | tf_op | source)
XLA Modules:
  0.0 143.3 jit_solution(7613068922668963565)
XLA Ops:
  0.0 141.4 %orbit_attention.1 = bf16[192,1536]{1,0:T(8,128)(2,1)} custom-call(bf16[3,192,1536]{2,1,0:T(8,128)(2,1)} %bitcast.6, s32[6,6,2,128]{3,2,1,0:T(2,128)} %bitcast.7), custom_call_target="tpu_custom_call" | custom-call | tf_op jit(solution)/shard_map/orbit_attention/pallas_call | solution.py:426
  141.4 1.9 %copy.4 = bf16[1,192,1536]{2,1,0:T(8,128)(2,1)} copy(bf16[1,192,1536]{2,1,0:T(8,128)(2,1)} %bitcast.5) | data formatting | bytes 1179648
